TPU v7x, 128 devices: a whole 4x4x4 slice. The times are simulated.
128 devices in a mesh: seq: 16 (over y, z), tp: 8 (over x, core).
Axes of the slice: x: 4, y: 4, z: 4, core: 2. Of those that a mesh axis runs over, the one named last changes fastest.
Arguments:
- queries: bfloat16 [2048, 8192], P('seq', 'tp'), may hold values from -8 to 8
- prompt_prefix_keys: bfloat16 [32768, 1024], P('seq', 'tp'), may hold values from -8 to 8
- prompt_prefix_values: bfloat16 [32768, 1024], P('seq', 'tp'), may hold values from -6 to 6
- continuation_keys: bfloat16 [2048, 1024], P('seq', 'tp'), may hold values from -8 to 8
- continuation_values: bfloat16 [2048, 1024], P('seq', 'tp'), may hold values from -6 to 6
- owners: int32 [64, 4], P('seq'), may hold values from 0 to 15, all different within a row; in each aligned block of 4 rows (0 to 3, 4 to 7, ...) at most 2 rows name the same one
- lengths: int32 [64], P('seq'), may hold values from 1 to 32, 1280 in all
- out_weight: bfloat16 [8192, 8192], P('tp'), may hold values from -2.5 to 2.5
Outputs:
- mixed: bfloat16 [2048, 8192], P(('seq', 'tp'))
Inputs may be any that keep to these rules, and one draw needn't show every extreme that they name: Each row names 4 different owners. Among the 4 branches of one index of seq no owner is named more than 2 times, and in every draw some owner is named exactly 2 times by the branches of some index. `lengths`: the largest length equals 32.
All inputs are finite; a program needn't handle non-finite values. No bound on the sum of `lengths` on one device may be relied on, other than what follows from the above.
Results may differ from a plain program's by a relative error of at most 0.0055.
Values may be sent and summed in bfloat16 or wider, within the bound.
A program may use at most 128 MiB of HBM per device.

v0:
```python
import jax
import jax.numpy as jnp
from jax import lax
from jax.sharding import PartitionSpec as P

HEAD_WIDTH = 128


MASKED_SCORE = -1e30


def attend(query_tile_rows, keys, value_rows, allowed):
    scores = jnp.einsum(
        "thgd,shd->hgts", query_tile_rows, keys, preferred_element_type=jnp.float32
    ) * HEAD_WIDTH ** (-0.5)
    if allowed is not None:
        scores = jnp.where(allowed, scores, MASKED_SCORE)
    top = jnp.max(scores, axis=-1, keepdims=True)
    prob = jnp.exp(scores - top)
    total = jnp.sum(prob, axis=-1, keepdims=True)
    weights = prob.astype(jnp.bfloat16)
    result = jnp.einsum(
        "hgts,shd->thgd", weights, value_rows, preferred_element_type=jnp.float32
    ) / jnp.transpose(total, (2, 0, 1, 3))
    return (result, top[..., 0] + jnp.log(total[..., 0]))


def body(
    queries,
    prompt_prefix_keys,
    prompt_prefix_values,
    continuation_keys,
    continuation_values,
    owners,
    lengths,
    out_weight,
):
    branches = owners.shape[0]
    suffix_len = queries.shape[0] // branches
    width = queries.shape[1]
    heads = width // HEAD_WIDTH
    kv_heads = prompt_prefix_keys.shape[1] // HEAD_WIDTH
    group_size = heads // kv_heads
    pool = prompt_prefix_keys.shape[0]
    local_q = queries.reshape(branches, suffix_len, kv_heads, group_size, HEAD_WIDTH)
    flat_q = queries.reshape(branches * suffix_len, kv_heads, group_size, HEAD_WIDTH)
    positions = jnp.arange(suffix_len, dtype=jnp.int32)
    allowed = (positions[None, None, :] <= positions[None, :, None]) & (
        positions[None, None, :] < lengths[:, None, None]
    )
    own_out, own_lse = jax.vmap(attend)(
        local_q,
        continuation_keys.reshape(branches, suffix_len, kv_heads, HEAD_WIDTH),
        continuation_values.reshape(branches, suffix_len, kv_heads, HEAD_WIDTH),
        allowed,
    )
    own_out = own_out.reshape(branches, suffix_len, heads, HEAD_WIDTH)
    own_lse = own_lse.reshape(branches, heads, suffix_len)
    initial = (own_lse, own_out, jnp.ones_like(own_lse))
    piece_keys = lax.all_gather(prompt_prefix_keys, "seq", axis=0, tiled=True)
    piece_values = lax.all_gather(prompt_prefix_values, "seq", axis=0, tiled=True)
    length = piece_keys.shape[0]
    parts = max(1, length // pool)
    span = length // parts
    key_blocks = piece_keys.reshape(parts, span, kv_heads, HEAD_WIDTH)
    value_blocks = piece_values.reshape(parts, span, kv_heads, HEAD_WIDTH)

    def visit(state, inputs):
        peak, numer, total = state
        keys, values_block, index = inputs
        owner = index * span // pool
        part_out, part_lse = attend(flat_q, keys, values_block, None)
        part_out = lax.optimization_barrier(part_out.astype(jnp.bfloat16)).astype(jnp.float32)
        part_out = part_out.reshape(branches, suffix_len, heads, HEAD_WIDTH)
        part_lse = jnp.transpose(part_lse.reshape(heads, branches, suffix_len), (1, 0, 2))
        listed = jnp.any(owners == owner, axis=1)
        part_lse = jnp.where(listed[:, None, None], part_lse, MASKED_SCORE)
        new_peak = jnp.maximum(peak, part_lse)
        old_scale = jnp.exp(peak - new_peak)
        new_scale = jnp.exp(part_lse - new_peak)
        numer = (
            numer * jnp.transpose(old_scale, (0, 2, 1))[..., None]
            + part_out * jnp.transpose(new_scale, (0, 2, 1))[..., None]
        )
        total = total * old_scale + new_scale
        return ((new_peak, numer, total), None)

    state, unused = lax.scan(
        visit, initial, (key_blocks, value_blocks, jnp.arange(parts, dtype=jnp.int32))
    )
    peak, numer, total = state
    merged = numer / jnp.transpose(total, (0, 2, 1))[..., None]
    attention = merged.reshape(branches * suffix_len, width).astype(jnp.bfloat16)
    mixed = lax.psum_scatter(
        jnp.dot(attention, out_weight, preferred_element_type=jnp.float32),
        "tp",
        scatter_dimension=0,
        tiled=True,
    )
    return mixed.astype(jnp.bfloat16)


def solution(mesh):
    in_specs = (
        P("seq", "tp"),
        P("seq", "tp"),
        P("seq", "tp"),
        P("seq", "tp"),
        P("seq", "tp"),
        P("seq", None),
        P("seq"),
        P("tp", None),
    )
    out_specs = P(("seq", "tp"), None)
    return jax.shard_map(body, mesh=mesh, in_specs=in_specs, out_specs=out_specs, check_vma=False)
```

profile of v0, /device:TPU:1, one launch (start us, length us, event | category | flops | bytes accessed | tf_op | source)
XLA Modules:
  0.0 359.2 jit_solution(15249081832799426976)
XLA Ops:
  13.4 70.2 %all-gather.3.cloned.1.call-done = bf16[32768,128]{1,0:T(8,128)(2,1)} async-done(((bf16[2048,128]{1,0:T(8,128)(2,1)}), bf16[32768,128]{1,0:T(8,128)(2,1)}) %all-gather.3.cloned.1.call-update) | async-done | bytes 8388624 | tf_op jit(solution)/shard_map/all_gather | solution.py:60
  83.6 72.6 %all-gather.5.cloned.1.call-done = bf16[32768,128]{1,0:T(8,128)(2,1)} async-done(((bf16[2048,128]{1,0:T(8,128)(2,1)}), bf16[32768,128]{1,0:T(8,128)(2,1)}) %all-gather.5.cloned.1.call-update) | async-done | bytes 8388624 | tf_op jit(solution)/shard_map/all_gather | solution.py:61
  156.2 149.7 %while.17 = (s32[]{:T(128)}, f32[4,8,32]{1,2,0:T(8,128)S(1)}, f32[4,32,8,128]{3,2,1,0:T(8,128)S(1)}, f32[4,8,32]{1,2,0:T(8,128)S(1)}, s32[16]{0:T(128)S(1)}, /*i...) while((s32[]{:T(128)}, f32[4,8,32]{1,2,0:T(8,128)S(1)}, ...), condition=%wide.region_6.7_spmd.clone, body=%wide.region_2.6_spmd.clone.sunk | while | flops 1091183616 | bytes 29196700 | solution.py:88
  161.9 2.7 fusion.55
  171.2 2.7 fusion.55
  180.6 2.7 fusion.55
  186.3 2.3 bitcast_reduce_fusion.2
  189.9 2.7 fusion.55
  199.3 2.7 fusion.55
  205.0 2.3 bitcast_reduce_fusion.2
  208.7 2.7 fusion.55
  218.0 2.7 fusion.55
  223.7 2.3 bitcast_reduce_fusion.2
  227.4 2.7 fusion.55
  236.7 2.7 fusion.55
  246.1 2.7 fusion.55
  255.4 2.7 fusion.55
  264.8 2.7 fusion.55
  274.1 2.7 fusion.55
  283.5 2.7 fusion.55
  292.9 2.7 fusion.55
  302.2 2.7 fusion.55
  306.1 10.1 %fusion.36 = f32[128,8192]{1,0:T(8,128)} fusion(bf16[1024,8192]{1,0:T(8,128)(2,1)} %param.17, bf16[16,8,8,128]{3,2,1,0:T(8,128)(2,1)S(1)} %bitcast.162), kind=kOutput, calls=%fused_computation.41 | convolution fusion | flops 2147483648 | bytes 21233664 | tf_op jit(solution)/shard_map/dot_general | solution.py:95
  316.2 34.7 %reduce-scatter.2.cloned.1.call-done = f32[16,8192]{1,0:T(8,128)} async-done(((f32[128,8192]{1,0:T(8,128)}), f32[16,8192]{1,0:T(8,128)}) %reduce-scatter.2.cloned.1.call-update) | async-done | bytes 524304 | tf_op jit(solution)/shard_map/reduce_scatter | solution.py:94
  (197 shorter events, 97.3 us)
Async XLA Ops:
  6.5 6.1 %copy-start = (bf16[128,128]{1,0:T(8,128)(2,1)S(1)}, bf16[128,128]{1,0:T(8,128)(2,1)}, u32[]{:S(2)}) copy-start(bf16[128,128]{1,0:T(8,128)(2,1)} %param.14) | copy-start | bytes 98308
  6.5 77.1 %all-gather.3.cloned.1.call-start = ((), (), s32[]{:S(2)}) async-start(), calls=%async_computation.1 | async-start | bytes 8912896 | tf_op jit(solution)/shard_map/all_gather | solution.py:60
  7.3 149.0 %all-gather.5.cloned.1.call-start = ((), (), s32[]{:S(2)}) async-start(), calls=%async_computation.2 | async-start | bytes 8912896 | tf_op jit(solution)/shard_map/all_gather | solution.py:61
  8.0 342.9 %reduce-scatter.2.cloned.1.call-start = ((), (), s32[]{:S(2)}) async-start(), calls=%async_computation.3 | async-start | bytes 4718592 | tf_op jit(solution)/shard_map/reduce_scatter | solution.py:94
Sparse Core Ops, SparseCore 0:
  9.5 74.0 all-gather.2
  85.8 70.4 all-gather.4
  316.3 34.5 reduce-scatter.1
where the time goes:
time: 364 us; the launch traced here: 359 us
  waiting for transfers between devices  179 us (49%)
  matrix products  92.2 us (25%)
  other arithmetic  47.4 us (13%)
  local copies, waits for them, and re-layouts  16.9 us (5%)
  between operations  13.2 us (4%)
  loops' own time  10.4 us (3%)
    all_gather x1, waiting for transfers between devices, body(): lax.all_gather(prompt_prefix_values, 'seq', axis=0, tiled=True)  72.6 us
    all_gather x1, waiting for transfers between devices, body(): piece_keys = lax.all_gather(prompt_prefix_keys, 'seq', axis=0, tiled=True)  70.2 us
    dot_general x17, matrix products, attend(): jnp.einsum('hgts,shd->thgd', weights, value_rows, preferred_element_type=...  44.1 us
    dot_general x17, matrix products, attend(): jnp.einsum('thgd,shd->hgts', query_tile_rows, keys, preferred_element_typ...  38 us
    reduce_scatter x1, waiting for transfers between devices, body(): lax.psum_scatter(jnp.dot(attention, out_weight, preferred_element_type=jn...  34.7 us
    reduce_sum x17, other arithmetic, attend(): total = jnp.sum(prob, axis=-1, keepdims=True)  22.2 us
    reduce_or x16, other arithmetic, visit(): listed = jnp.any(owners == owner, axis=1)  12.8 us
    another operation x1, loops' own time, body(): lax.scan(visit, initial, (key_blocks, value_blocks, jnp.arange(parts, dty...  10.4 us
  transfers between devices with their start and end apart: 3, of which 3 were waited for; matrix products, arithmetic and copies ran while one was open for 1% of the time, Pallas kernels for 0%

commit v1 on v0

v1 whole, which is shorter than its diff:
```python
import functools

import jax
import jax.numpy as jnp
from jax import lax
from jax.experimental import pallas as pl
from jax.experimental.pallas import tpu as pltpu
from jax.sharding import PartitionSpec as P

HEAD = 128
SLOTS = 32
BRANCHES = 4
FAN = 4
HEADS = 8
COLS = HEADS * SLOTS
HALF = 1024
STRIP = 512
CHUNKS = 8
LOG2E = 1.4426950408889634
SCALE = HEAD**-0.5 * LOG2E
LOW = -1e30
MESH = pl.DeviceIdType.MESH
NT = (((1,), (1,)), ((), ()))
NN = (((1,), (0,)), ((), ()))


def dot(a, b, dims):
    return lax.dot_general(a, b, dims, preferred_element_type=jnp.float32)


def await_bytes(ref, sem):
    pltpu.make_async_copy(ref, ref, sem).wait()


def kernel(
    q_hbm, k_hbm, v_hbm, ck_ref, cv_ref, owners_ref, lengths_ref, w_hbm,
    out_ref,
    w_buf, kp, vp, v_own, qbuf, qs, own_vec, own_buf, raw, tab, inv,
    s_a, s_b, m_ref, l_ref, acc, own_m, own_l, own_acc,
    ret, ret_lse, back, back_lse, attn,
    part, total, pair_send, pair_recv, d_send, d_recv, r_send, r_recv,
    loc_sem, q_ssem, q_rsem, o_ssem, o_rsem, kv_ssem, kv_rsem,
    ret_ssem, ret_rsem, pair_ssem, pair_rsem, d_ssem, d_rsem, r_ssem, r_rsem,
):
    seq = lax.axis_index("seq")
    tp = lax.axis_index("tp")
    y, z = lax.div(seq, 4), lax.rem(seq, 4)
    x, core = lax.div(tp, 2), lax.rem(tp, 2)
    kv_pos = (1 - core) * z + core * y
    q_pos = (1 - core) * y + core * z

    def kv_seq(step):
        a = lax.rem(kv_pos + step, 4)
        return (1 - core) * (q_pos * 4 + a) + core * (a * 4 + q_pos)

    def q_seq(step):
        a = lax.rem(q_pos + step, 4)
        return (1 - core) * (a * 4 + kv_pos) + core * (kv_pos * 4 + a)

    kv_right, kv_left = (kv_seq(1), tp), (kv_seq(3), tp)
    peers = {1: (q_seq(3), tp), 2: (q_seq(1), tp), 3: (q_seq(2), tp)}
    mirror = {1: 2, 2: 1, 3: 3}
    partner = (seq, x * 2 + 1 - core)
    x_right = (seq, lax.rem(x + 1, 4) * 2 + core)
    x_left = (seq, lax.rem(x + 3, 4) * 2 + core)
    everyone = (kv_right, kv_left, peers[1], peers[2], peers[3], partner, x_right, x_left)

    def remote(src, dst, ssem, rsem, device):
        return pltpu.make_async_remote_copy(
            src_ref=src, dst_ref=dst, send_sem=ssem, recv_sem=rsem, device_id=device, device_id_type=MESH
        )

    barrier = pltpu.get_barrier_semaphore()
    for device in everyone:
        pl.semaphore_signal(barrier, inc=1, device_id=device, device_id_type=MESH)

    copy_v = pltpu.make_async_copy(v_hbm, v_own, loc_sem.at[0])
    copy_v.start()
    copy_q = pltpu.make_async_copy(q_hbm, qbuf.at[0], q_rsem.at[0])
    copy_q.start()
    copy_k = [
        pltpu.make_async_copy(k_hbm.at[pl.ds(h * HALF, HALF), :], kp.at[h], loc_sem.at[1 + h]) for h in range(2)
    ]
    for c in copy_k:
        c.start()

    rows = lax.broadcasted_iota(jnp.int32, (8, 128), 0)
    lanes = lax.broadcasted_iota(jnp.int32, (8, 128), 1)
    vec = jnp.zeros((8, 128), jnp.int32)
    for b in range(BRANCHES):
        for f in range(FAN):
            vec = jnp.where((rows == b) & (lanes == f), owners_ref[b, f], vec)
    own_vec[...] = vec
    copy_o = pltpu.make_async_copy(own_vec, own_buf.at[0], o_rsem.at[0])
    copy_o.start()

    pl.semaphore_wait(barrier, len(everyone))

    sends = []
    for j in (3, 1, 2):
        sends.append(remote(own_vec, own_buf.at[mirror[j]], o_ssem.at[j], o_rsem.at[mirror[j]], peers[j]))
        sends[-1].start()
    for j in (1, 2, 3):
        sends.append(remote(q_hbm, qbuf.at[mirror[j]], q_ssem.at[j], q_rsem.at[mirror[j]], peers[j]))
        sends[-1].start()
    routes = ((0, 2, kv_right), (1, 3, kv_left), (1, 4, kv_right), (0, 5, kv_left))

    def kv_send(h, piece, device, which):
        src, dst = (kp, kp) if which == 0 else (vp, vp)
        return remote(src.at[h], dst.at[piece], kv_ssem.at[which, piece], kv_rsem.at[which, piece], device)

    for c in copy_k:
        c.wait()
    for h, piece, device in routes[:2]:
        sends.append(kv_send(h, piece, device, 0))
        sends[-1].start()
    copy_v.wait()
    for h in range(2):
        vp[h] = jnp.transpose(v_own[pl.ds(h * HALF, HALF), :].astype(jnp.float32)).astype(jnp.bfloat16)
    for h, piece, device in routes[:2]:
        sends.append(kv_send(h, piece, device, 1))
        sends[-1].start()
    for which in range(2):
        for h, piece, device in routes[2:]:
            sends.append(kv_send(h, piece, device, which))
            sends[-1].start()
    copy_w = pltpu.make_async_copy(w_hbm, w_buf, loc_sem.at[3])
    copy_w.start()

    m_ref[...] = jnp.full(m_ref.shape, LOW, jnp.float32)
    l_ref[...] = jnp.zeros(l_ref.shape, jnp.float32)
    acc[...] = jnp.zeros(acc.shape, jnp.float32)

    def slot_of(o, j, k):
        return o * 8 + j * 2 + k

    def column_max(scores):
        return jnp.max(scores.reshape(scores.shape[0] // 64, 64, COLS), axis=0)

    def advance(ahead, dst, behind, src, top):
        if ahead is not None:
            piece, o, j, k = ahead
            q_now = qs[j * BRANCHES + tab[slot_of(o, j, k)]]
        if behind is not None:
            piece2, o2, j2, k2 = behind
            s2 = slot_of(o2, j2, k2)
            old = m_ref[s2]
            new = jnp.maximum(old, top)
            shrink = jnp.exp2(old - new)
        best = gain = None
        for c in range(HALF // STRIP):
            span = pl.ds(c * STRIP, STRIP)
            if ahead is not None:
                k_now = kp[piece, span, :]
                scores = dot(jnp.concatenate([k_now, k_now], axis=1), q_now, NT)
            if behind is not None:
                weights = jnp.exp2(src[span, :] - new).astype(jnp.bfloat16)
            if ahead is not None:
                dst[span, :] = scores
                here = column_max(scores)
                best = here if best is None else jnp.maximum(best, here)
            if behind is not None:
                values = jnp.concatenate([vp[piece2, :, span], jnp.ones((16, STRIP), jnp.bfloat16)], axis=0)
                term = dot(values, weights, NN)
                gain = term if gain is None else gain + term
        if behind is not None:
            m_ref[s2] = new
            l_ref[s2] = l_ref[s2] * shrink + gain[HEAD : HEAD + 1]
            acc[s2] = acc[s2] * shrink + gain[:HEAD]
        if ahead is not None:
            return jnp.max(best, axis=0, keepdims=True)

    def four(j, o, first_piece):
        steps = [(first_piece + h, o, j, k) for h in range(2) for k in range(2)]
        bufs = (s_a, s_b)
        top = advance(steps[0], bufs[0], None, None, None)
        for t in range(4):
            ahead = steps[t + 1] if t < 3 else None
            top = advance(ahead, bufs[(t + 1) % 2], steps[t], bufs[t % 2], top)

    group = [seq, kv_seq(3), kv_seq(1), kv_seq(2)]

    def source(j, carry):
        await_bytes(own_buf.at[j], o_rsem.at[j])
        copy = pltpu.make_async_copy(own_buf.at[j], raw, loc_sem.at[4])
        copy.start()
        copy.wait()
        for o in range(4):
            count, first, second = jnp.int32(0), jnp.int32(0), jnp.int32(0)
            for b in range(BRANCHES):
                hit = raw[b, 0] == group[o]
                for f in range(1, FAN):
                    hit = hit | (raw[b, f] == group[o])
                inv[(o * 4 + j) * BRANCHES + b] = jnp.where(hit & (count < 2), count, -1)
                first = jnp.where(hit & (count == 0), b, first)
                second = jnp.where(hit & (count == 1), b, second)
                count = count + hit.astype(jnp.int32)
            tab[slot_of(o, j, 0)] = first
            tab[slot_of(o, j, 1)] = second
        await_bytes(qbuf.at[j], q_rsem.at[j])
        for b in range(BRANCHES):
            stacked = jnp.concatenate([qbuf[j, b, :, pl.ds(h * HEAD, HEAD)] for h in range(HEADS)], axis=0)
            exact = stacked.astype(jnp.float32) * SCALE
            high = exact.astype(jnp.bfloat16)
            qs[j * BRANCHES + b, :, :HEAD] = high
            qs[j * BRANCHES + b, :, HEAD:] = (exact - high.astype(jnp.float32)).astype(jnp.bfloat16)
        four(j, 0, 0)
        return carry

    lax.fori_loop(0, 4, source, 0)

    row = lax.broadcasted_iota(jnp.int32, (BRANCHES * SLOTS, COLS), 0)
    slot = lax.rem(lax.broadcasted_iota(jnp.int32, (BRANCHES * SLOTS, COLS), 1), SLOTS)
    ck = ck_ref[...]
    ck2 = jnp.concatenate([ck, ck], axis=1)
    cv_t = jnp.transpose(cv_ref[...].astype(jnp.float32)).astype(jnp.bfloat16)
    for b in range(BRANCHES):
        key = row - b * SLOTS
        allowed = (key >= 0) & (key <= slot) & (key < lengths_ref[b])
        scores = jnp.where(allowed, dot(ck2, qs[b], NT), LOW)
        top = jnp.max(scores, axis=0, keepdims=True)
        prob = jnp.where(allowed, jnp.exp2(scores - top), 0.0)
        own_m[b] = top
        own_l[b] = jnp.sum(prob, axis=0, keepdims=True)
        own_acc[b] = dot(cv_t, prob.astype(jnp.bfloat16), NN)

    for d in range(2):
        for piece in (2 + 2 * d, 3 + 2 * d):
            for which, buf in ((0, kp), (1, vp)):
                await_bytes(buf.at[piece], kv_rsem.at[which, piece])
                if d == 0:
                    sends.append(kv_send(piece, piece + 4, kv_right if piece == 2 else kv_left, which))
                    sends[-1].start()

        def step_of(t, d=d):
            return (2 + 2 * d + lax.div(t, 8), 1 + lax.div(t, 8), lax.div(lax.rem(t, 8), 2), lax.rem(t, 2))

        def two(i, top, step_of=step_of):
            t = 2 * i
            top = advance(step_of(t + 1), s_b, step_of(t), s_a, top)
            return advance(step_of(lax.rem(t + 2, 16)), s_a, step_of(t + 1), s_b, top)

        lax.fori_loop(0, 8, two, advance(step_of(jnp.int32(0)), s_a, None, None, None))

    for piece in (6, 7):
        for which, buf in ((0, kp), (1, vp)):
            await_bytes(buf.at[piece], kv_rsem.at[which, piece])

    def ret_copies(j):
        return (
            remote(ret.at[j], back.at[mirror[j]], ret_ssem.at[0, j], ret_rsem.at[0, mirror[j]], peers[j]),
            remote(ret_lse.at[j], back_lse.at[mirror[j]], ret_ssem.at[1, j], ret_rsem.at[1, mirror[j]], peers[j]),
        )

    def finish(i, carry):
        j = 3 - i
        four(j, 3, 6)
        for b in range(BRANCHES):
            slots, tops, sums, oks = [], [], [], []
            for o in range(4):
                place = inv[(o * 4 + j) * BRANCHES + b]
                ok = place >= 0
                s = slot_of(o, j, jnp.where(ok, place, 0))
                slots.append(s)
                oks.append(ok)
                tops.append(jnp.where(ok, m_ref[s], LOW))
                sums.append(l_ref[s])
            peak = functools.reduce(jnp.maximum, tops)
            scales = [jnp.where(ok, jnp.exp2(t - peak), 0.0) for ok, t in zip(oks, tops)]
            denom = sum(a * l for a, l in zip(scales, sums))
            any_ok = denom > 0.0
            safe = jnp.where(any_ok, denom, 1.0)
            merged = sum(acc[s] * (a / safe) for s, a in zip(slots, scales))
            ret[j, b] = merged.astype(jnp.bfloat16)
            ret_lse[j, b : b + 1, :] = jnp.where(any_ok, peak + jnp.log(safe) * LOG2E, LOW)
        for n in (1, 2, 3):

            @pl.when(j == n)
            def _():
                for c in ret_copies(n):
                    c.start()

        return carry

    lax.fori_loop(0, 4, finish, 0)
    for n in (1, 2, 3):
        for c in ret_copies(n):
            c.wait_recv()

    for b in range(BRANCHES):
        lses = [own_m[b] + jnp.log(own_l[b]) * LOG2E, ret_lse[0, b : b + 1, :]]
        lses += [back_lse[n, b : b + 1, :] for n in (1, 2, 3)]
        peak = functools.reduce(jnp.maximum, lses)
        scales = [jnp.exp2(t - peak) for t in lses]
        denom = sum(scales)
        merged = own_acc[b] * (scales[0] / (denom * own_l[b]))
        outs = [ret[0, b]] + [back[n, b] for n in (1, 2, 3)]
        for a, o in zip(scales[1:], outs):
            merged = merged + o.astype(jnp.float32) * (a / denom)
        turned = jnp.transpose(merged).astype(jnp.bfloat16)
        for h in range(HEADS):
            attn[b * SLOTS : (b + 1) * SLOTS, h * HEAD : (h + 1) * HEAD] = turned[h * SLOTS : (h + 1) * SLOTS, :]
    copy_w.wait()

    width = w_buf.shape[1] // CHUNKS
    mid = width // 2
    share = part.shape[2]
    right, left, far = lax.rem(x + 1, 4), lax.rem(x + 3, 4), lax.rem(x + 2, 4)

    def pair_copy(n):
        return remote(pair_send.at[n], pair_recv.at[n], pair_ssem.at[n], pair_rsem.at[n], partner)

    def d_copies(n):
        return tuple(
            remote(d_send.at[n, i], d_recv.at[n, i], d_ssem.at[n, i], d_rsem.at[n, i], device)
            for i, device in ((0, x_right), (1, x_left))
        )

    def r_copies(n):
        return tuple(
            remote(r_send.at[n, i], r_recv.at[n, i], r_ssem.at[n, i], r_rsem.at[n, i], device)
            for i, device in ((0, x_right), (1, x_left))
        )

    def project(n):
        columns = pl.ds(pl.multiple_of(n * width, width), width)
        part[n] = dot(attn[...], w_buf[:, columns], NN).reshape(8, share, width)
        for i in range(4):
            pair_send[n, i] = part[n, 2 * i + 1 - core].astype(jnp.bfloat16)
        pair_copy(n).start()

    def pair_sum(n):
        pair_copy(n).wait_recv()
        for i in range(4):
            total[n, i] = part[n, 2 * i + core] + pair_recv[n, i].astype(jnp.float32)
        d_send[n, 0] = total[n, far, :, :mid].astype(jnp.bfloat16)
        d_send[n, 1] = total[n, far, :, mid:].astype(jnp.bfloat16)
        for c in d_copies(n):
            c.start()

    def ring_sum(n):
        for c in d_copies(n):
            c.wait_recv()
        r_send[n, 0, :, :mid] = (total[n, right, :, :mid] + d_recv[n, 0].astype(jnp.float32)).astype(jnp.bfloat16)
        r_send[n, 0, :, mid:] = total[n, right, :, mid:].astype(jnp.bfloat16)
        r_send[n, 1, :, :mid] = total[n, left, :, :mid].astype(jnp.bfloat16)
        r_send[n, 1, :, mid:] = (total[n, left, :, mid:] + d_recv[n, 1].astype(jnp.float32)).astype(jnp.bfloat16)
        for c in r_copies(n):
            c.start()

    def last_sum(n):
        for c in r_copies(n):
            c.wait_recv()
        columns = pl.ds(pl.multiple_of(n * width, width), width)
        out_ref[:, columns] = (
            total[n, x] + r_recv[n, 0].astype(jnp.float32) + r_recv[n, 1].astype(jnp.float32)
        ).astype(jnp.bfloat16)

    def tail(i, carry):
        for lag, stage in enumerate((project, pair_sum, ring_sum, last_sum)):
            n = i - lag

            @pl.when((n >= 0) & (n < CHUNKS))
            def _():
                stage(n)

        return carry

    lax.fori_loop(0, CHUNKS + 3, tail, 0)

    for c in sends:
        c.wait_send()
    for n in (1, 2, 3):
        for c in ret_copies(n):
            c.wait_send()

    def drain(n, carry):
        pair_copy(n).wait_send()
        for c in d_copies(n) + r_copies(n):
            c.wait_send()
        return carry

    lax.fori_loop(0, CHUNKS, drain, 0)


def body(queries, keys, values, own_keys, own_values, owners, lengths, out_weight):
    share = queries.shape[0] // 8
    depth, columns = out_weight.shape
    width = columns // CHUNKS
    mid = width // 2
    bf16, f32, i32 = jnp.bfloat16, jnp.float32, jnp.int32
    vmem = pltpu.VMEM
    dma = pltpu.SemaphoreType.DMA
    anywhere = pl.BlockSpec(memory_space=pl.ANY)
    inside = pl.BlockSpec(memory_space=pltpu.VMEM)
    scalars = pl.BlockSpec(memory_space=pltpu.SMEM)
    return pl.pallas_call(
        kernel,
        out_shape=jax.ShapeDtypeStruct((share, columns), bf16),
        in_specs=[anywhere, anywhere, anywhere, inside, inside, scalars, scalars, anywhere],
        out_specs=inside,
        scratch_shapes=[
            vmem((depth, columns), bf16),
            vmem((8, HALF, HEAD), bf16),
            vmem((8, HEAD, HALF), bf16),
            vmem((2 * HALF, HEAD), bf16),
            vmem((4, BRANCHES, SLOTS, HEADS * HEAD), bf16),
            vmem((4 * BRANCHES, COLS, 2 * HEAD), bf16),
            vmem((8, 128), i32),
            vmem((4, 8, 128), i32),
            pltpu.SMEM((8, 128), i32),
            pltpu.SMEM((32,), i32),
            pltpu.SMEM((64,), i32),
            vmem((HALF, COLS), f32),
            vmem((HALF, COLS), f32),
            vmem((32, 1, COLS), f32),
            vmem((32, 1, COLS), f32),
            vmem((32, HEAD, COLS), f32),
            vmem((BRANCHES, 1, COLS), f32),
            vmem((BRANCHES, 1, COLS), f32),
            vmem((BRANCHES, HEAD, COLS), f32),
            vmem((4, BRANCHES, HEAD, COLS), bf16),
            vmem((4, 8, COLS), f32),
            vmem((4, BRANCHES, HEAD, COLS), bf16),
            vmem((4, 8, COLS), f32),
            vmem((BRANCHES * SLOTS, depth), bf16),
            vmem((CHUNKS, 8, share, width), f32),
            vmem((CHUNKS, 4, share, width), f32),
            vmem((CHUNKS, 4, share, width), bf16),
            vmem((CHUNKS, 4, share, width), bf16),
            vmem((CHUNKS, 2, share, mid), bf16),
            vmem((CHUNKS, 2, share, mid), bf16),
            vmem((CHUNKS, 2, share, width), bf16),
            vmem((CHUNKS, 2, share, width), bf16),
            dma((5,)),
            dma((4,)), dma((4,)), dma((4,)), dma((4,)),
            dma((2, 8)), dma((2, 8)),
            dma((2, 4)), dma((2, 4)),
            dma((CHUNKS,)), dma((CHUNKS,)),
            dma((CHUNKS, 2)), dma((CHUNKS, 2)), dma((CHUNKS, 2)), dma((CHUNKS, 2)),
        ],
        compiler_params=pltpu.CompilerParams(
            collective_id=0, has_side_effects=True, vmem_limit_bytes=58 * 1024 * 1024
        ),
        name="branch_attention",
    )(
        queries.reshape(BRANCHES, SLOTS, queries.shape[1]),
        keys, values, own_keys, own_values, owners, lengths, out_weight,
    )


def solution(mesh):
    in_specs = (
        P("seq", "tp"),
        P("seq", "tp"),
        P("seq", "tp"),
        P("seq", "tp"),
        P("seq", "tp"),
        P("seq", None),
        P("seq"),
        P("tp", None),
    )
    out_specs = P(("seq", "tp"), None)
    return jax.shard_map(body, mesh=mesh, in_specs=in_specs, out_specs=out_specs, check_vma=False)
```

time: 364 us -> 74.7 us (0.21); the launches traced: 359 us -> 74.5 us
  waiting for transfers between devices: 179 us -> 0 us
  matrix products: 92.2 us -> 0 us
  Pallas kernels: 0 us -> 72.8 us
  other arithmetic: 47.4 us -> 0 us
  local copies, waits for them, and re-layouts: 16.9 us -> 1.67 us
  between operations: 13.2 us -> 0.01 us
  loops' own time: 10.4 us -> 0 us
    all_gather x2 -> x0, waiting for transfers between devices: 143 us -> none  [the longest x1 72.6 us: body(): lax.all_gather(prompt_prefix_values, 'seq', axis=0, tiled=True)]
    dot_general x35 -> x0, matrix products: 92.2 us -> none  [the longest x17 44.1 us: attend(): jnp.einsum('hgts,shd->thgd', weights, value_rows, preferred_element_type=...]
    pallas_call x0 -> x1, Pallas kernels: none -> 72.8 us  [body(): pl.pallas_call(kernel, out_shape=jax.ShapeDtypeStruct((share, columns), b...]
    reduce_scatter x1 -> x0, waiting for transfers between devices: 34.7 us -> none  [body(): lax.psum_scatter(jnp.dot(attention, out_weight, preferred_element_type=jn...]
    reduce_sum x17 -> x0, other arithmetic: 22.2 us -> none  [attend(): total = jnp.sum(prob, axis=-1, keepdims=True)]
    reduce_or x16 -> x0, other arithmetic: 12.8 us -> none  [visit(): listed = jnp.any(owners == owner, axis=1)]
    another operation x1 -> x0, loops' own time: 10.4 us -> none  [body(): lax.scan(visit, initial, (key_blocks, value_blocks, jnp.arange(parts, dty...]
    dynamic_slice x16 -> x0, local copies, waits for them, and re-layouts: 9.3 us -> none  [body(): lax.scan(visit, initial, (key_blocks, value_blocks, jnp.arange(parts, dty...]
  transfers between devices with their start and end apart: 3 -> 0, of which waited for: 3 -> 0; matrix products, arithmetic and copies ran while one was open for 1% -> 0% of each run, Pallas kernels for 0% -> 0%
where the time goes in v1:
time: 74.7 us; the launch traced here: 74.5 us
  Pallas kernels  72.8 us (97%)
  local copies, waits for them, and re-layouts  1.67 us (2%)
    pallas_call x1, Pallas kernels, body(): pl.pallas_call(kernel, out_shape=jax.ShapeDtypeStruct((share, columns), b...  72.8 us
    unnamed x1, local copies, waits for them, and re-layouts  1.67 us

profile of v1, /device:TPU:1, one launch (start us, length us, event | category | flops | bytes accessed | tf_op | source)
XLA Modules:
  0.0 74.5 jit_solution(18139655086082436389)
XLA Ops:
  0.0 72.8 %branch_attention.1 = bf16[16,8192]{1,0:T(8,128)(2,1)} custom-call(bf16[4,32,1024]{2,1,0:T(8,128)(2,1)} %bitcast.1, bf16[2048,128]{1,0:T(8,128)(2,1)} %k_hbm.1, bf16[2048,128]{1,0:T(8,128)(2,1)} %v_hbm.1, bf16[128,128]{1,0:T(8,128)(2,1)} %ck_ref.1, bf16[128,128]{1,0:T(8,128)(2,1)} %cv_ref.1, s32[4,4]{1,0:T(4,128)} %owners_ref.1, s32[4]{0:T(128)} %lengths_ref.1, ...), custom_call_target="tpu_custom_call" | custom-call | tf_op jit(solution)/shard_map/branch_attention/pallas_call | solution.py:397
  72.8 1.7 %copy.10 = bf16[16,8192]{1,0:T(8,128)(2,1)} copy(bf16[16,8192]{1,0:T(8,128)(2,1)} %branch_attention.1) | data formatting | bytes 524288

commit v2 on v1

v2 whole, which is shorter than its diff:
```python
import functools

import jax
import jax.numpy as jnp
from jax import lax
from jax.experimental import pallas as pl
from jax.experimental.pallas import tpu as pltpu
from jax.sharding import PartitionSpec as P

HEAD = 128
SLOTS = 32
BRANCHES = 4
FAN = 4
HEADS = 8
COLS = HEADS * SLOTS
HALF = 1024
STRIP = 512
CHUNKS = 4
LAGS = (0, 1, 3, 5)
LOG2E = 1.4426950408889634
SCALE = HEAD**-0.5 * LOG2E
LOW = -1e30
MESH = pl.DeviceIdType.MESH
NT = (((1,), (1,)), ((), ()))
NN = (((1,), (0,)), ((), ()))


def dot(a, b, dims):
    return lax.dot_general(a, b, dims, preferred_element_type=jnp.float32)


def await_bytes(ref, sem):
    pltpu.make_async_copy(ref, ref, sem).wait()


def kernel(
    q_hbm, k_hbm, v_hbm, ck_ref, cv_ref, owners_ref, lengths_ref, w_hbm,
    out_ref,
    w_buf, kp, vp, v_own, qbuf, qs, own_vec, own_buf, raw, tab, inv,
    s_a, s_b, p_a, p_b, m_ref, l_ref, acc, own_m, own_l, own_acc,
    ret, ret_lse, back, back_lse, attn,
    part, total, pair_send, pair_recv, d_send, d_recv, r_send, r_recv,
    loc_sem, q_ssem, q_rsem, o_ssem, o_rsem, kv_ssem, kv_rsem,
    ret_ssem, ret_rsem, pair_ssem, pair_rsem, d_ssem, d_rsem, r_ssem, r_rsem,
):
    seq = lax.axis_index("seq")
    tp = lax.axis_index("tp")
    y, z = lax.div(seq, 4), lax.rem(seq, 4)
    x, core = lax.div(tp, 2), lax.rem(tp, 2)
    kv_pos = (1 - core) * z + core * y
    q_pos = (1 - core) * y + core * z

    def kv_seq(step):
        a = lax.rem(kv_pos + step, 4)
        return (1 - core) * (q_pos * 4 + a) + core * (a * 4 + q_pos)

    def q_seq(step):
        a = lax.rem(q_pos + step, 4)
        return (1 - core) * (a * 4 + kv_pos) + core * (kv_pos * 4 + a)

    kv_right, kv_left = (kv_seq(1), tp), (kv_seq(3), tp)
    peers = {1: (q_seq(3), tp), 2: (q_seq(1), tp), 3: (q_seq(2), tp)}
    mirror = {1: 2, 2: 1, 3: 3}
    partner = (seq, x * 2 + 1 - core)
    x_right = (seq, lax.rem(x + 1, 4) * 2 + core)
    x_left = (seq, lax.rem(x + 3, 4) * 2 + core)
    everyone = (kv_right, kv_left, peers[1], peers[2], peers[3], partner, x_right, x_left)

    def remote(src, dst, ssem, rsem, device):
        return pltpu.make_async_remote_copy(
            src_ref=src, dst_ref=dst, send_sem=ssem, recv_sem=rsem, device_id=device, device_id_type=MESH
        )

    barrier = pltpu.get_barrier_semaphore()
    for device in everyone:
        pl.semaphore_signal(barrier, inc=1, device_id=device, device_id_type=MESH)

    copy_v = pltpu.make_async_copy(v_hbm, v_own, loc_sem.at[0])
    copy_v.start()
    copy_q = pltpu.make_async_copy(q_hbm, qbuf.at[0], q_rsem.at[0])
    copy_q.start()
    copy_k = pltpu.make_async_copy(k_hbm, kp.at[pl.ds(0, 4)], loc_sem.at[1])
    copy_k.start()

    rows = lax.broadcasted_iota(jnp.int32, (8, 128), 0)
    lanes = lax.broadcasted_iota(jnp.int32, (8, 128), 1)
    vec = jnp.zeros((8, 128), jnp.int32)
    for b in range(BRANCHES):
        for f in range(FAN):
            vec = jnp.where((rows == b) & (lanes == f), owners_ref[b, f], vec)
    own_vec[...] = vec
    copy_o = pltpu.make_async_copy(own_vec, own_buf.at[0], o_rsem.at[0])
    copy_o.start()

    copy_v.wait()
    for n in (0, 2, 1, 3):
        vp[n] = jnp.transpose(v_own[pl.ds(n * STRIP, STRIP), :].astype(jnp.float32)).astype(jnp.bfloat16)
    pl.semaphore_wait(barrier, len(everyone))

    sends = []
    for j in (3, 1, 2):
        sends.append(remote(own_vec, own_buf.at[mirror[j]], o_ssem.at[j], o_rsem.at[mirror[j]], peers[j]))
        sends[-1].start()
    for j in (1, 2):
        sends.append(remote(q_hbm, qbuf.at[mirror[j]], q_ssem.at[j], q_rsem.at[mirror[j]], peers[j]))
        sends[-1].start()
    q_relay = [
        remote(qbuf.at[1, pl.ds(0, 2)], qbuf.at[3, pl.ds(0, 2)], q_ssem.at[3], q_rsem.at[3], peers[2]),
        remote(qbuf.at[2, pl.ds(2, 2)], qbuf.at[3, pl.ds(2, 2)], q_ssem.at[4], q_rsem.at[4], peers[1]),
    ]

    def kv_send(src, dst, count, device, which):
        buf = (kp, vp)[which]
        source_ref = k_hbm if which == 0 and src < 4 else buf
        return remote(
            source_ref.at[pl.ds(src, count)], buf.at[pl.ds(dst, count)],
            kv_ssem.at[which, dst], kv_rsem.at[which, dst], device,
        )

    def kv_await(quarter, count):
        for which, buf in ((0, kp), (1, vp)):
            await_bytes(buf.at[pl.ds(quarter, count)], kv_rsem.at[which, quarter])

    opening = [
        [kv_send(i, 4 + i, 1, kv_right, which) for which in range(2)]
        + [kv_send(2 + i, 6 + i, 1, kv_left, which) for which in range(2)]
        for i in range(2)
    ]
    closing = [
        kv_send(src, dst, 2, device, which)
        for which in range(2) for src, dst, device in ((2, 8, kv_right), (0, 10, kv_left))
    ]
    relay = [
        [kv_send(4 + i, 12 + i, 1, kv_right, which) for which in range(2)]
        + [kv_send(6 + i, 14 + i, 1, kv_left, which) for which in range(2)]
        for i in range(2)
    ]
    sends += q_relay + opening[0] + opening[1] + closing + relay[0] + relay[1]

    copy_k.wait()
    copy_w = pltpu.make_async_copy(w_hbm, w_buf, loc_sem.at[2])
    copy_w.start()

    m_ref[...] = jnp.full(m_ref.shape, LOW, jnp.float32)
    l_ref[...] = jnp.zeros(l_ref.shape, jnp.float32)
    acc[...] = jnp.zeros(acc.shape, jnp.float32)

    def slot_of(o, j, k):
        return o * 8 + j * 2 + k

    def stage(ahead, s_out, middle, top, s_in, p_out, behind, shrink, p_in):
        best = gain = next_shrink = None
        if ahead is not None:
            quarter, gap, j, s0 = ahead
            q_now = qs[j * BRANCHES + tab[s0]]
        if middle is not None:
            mid_slot = middle[3]
            old = m_ref[mid_slot]
            new = jnp.maximum(old, jnp.max(top, axis=0, keepdims=True))
            next_shrink = jnp.exp2(old - new)
            m_ref[mid_slot] = new
        for c in range(2):
            span = pl.ds(c * STRIP, STRIP)
            if ahead is not None:
                k_now = kp[quarter + c * gap]
                scores = dot(jnp.concatenate([k_now, k_now], axis=1), q_now, NT)
            if behind is not None:
                values = jnp.concatenate([vp[behind[0] + c * behind[1]], jnp.ones((16, STRIP), jnp.bfloat16)], axis=0)
                term = dot(values, p_in[span, :], NN)
                gain = term if gain is None else gain + term
            if middle is not None:
                p_out[span, :] = jnp.exp2(s_in[span, :] - new).astype(jnp.bfloat16)
            if ahead is not None:
                s_out[span, :] = scores
                here = jnp.max(scores.reshape(STRIP // 64, 64, COLS), axis=0)
                best = here if best is None else jnp.maximum(best, here)
        if behind is not None:
            s2 = behind[3]
            l_ref[s2] = l_ref[s2] * shrink + gain[HEAD : HEAD + 1]
            acc[s2] = acc[s2] * shrink + gain[:HEAD]
        if best is not None:
            best = jnp.max(best.reshape(8, 8, COLS), axis=0)
        return best, next_shrink

    def step_of(i, u):
        own = 1 - lax.div(i + (6 if u < 4 else 7), 8)
        piece = (1 - own) * (i - (2 if u < 4 else 1))
        far = lax.div(piece, 4)
        quarter = own * 2 * (u % 4 // 2) + (1 - own) * (4 + 2 * piece)
        owner = (1 - own) * ((1 - far) * (1 + lax.rem(piece, 2)) + 3 * far)
        j = own * (2 * i + (1 if u < 4 else 2)) + (1 - own) * ((2 if u < 4 else 0) + u % 4 // 2)
        return quarter, 1 + far, j, slot_of(owner, j, u % 2)

    def last_step(u):
        return 13, 2, 3 - u // 2, slot_of(3, 3 - u // 2, u % 2)

    scores_of, probs_of = (s_a, s_b), (p_a, p_b)

    def advance(u, ahead, middle, behind, top, shrink):
        return stage(
            ahead, scores_of[u % 2], middle, top, scores_of[(u + 1) % 2], probs_of[(u + 1) % 2],
            behind, shrink, probs_of[u % 2],
        )

    group = [seq, kv_seq(3), kv_seq(1), kv_seq(2)]

    def own_rows():
        row = lax.broadcasted_iota(jnp.int32, (BRANCHES * SLOTS, COLS), 0)
        slot = lax.rem(lax.broadcasted_iota(jnp.int32, (BRANCHES * SLOTS, COLS), 1), SLOTS)
        ck = ck_ref[...]
        ck2 = jnp.concatenate([ck, ck], axis=1)
        cv_t = jnp.transpose(cv_ref[...].astype(jnp.float32)).astype(jnp.bfloat16)
        for b in range(BRANCHES):
            key = row - b * SLOTS
            allowed = (key >= 0) & (key <= slot) & (key < lengths_ref[b])
            scores = jnp.where(allowed, dot(ck2, qs[b], NT), LOW)
            top = jnp.max(scores, axis=0, keepdims=True)
            prob = jnp.where(allowed, jnp.exp2(scores - top), 0.0)
            own_m[b] = top
            own_l[b] = jnp.sum(prob, axis=0, keepdims=True)
            own_acc[b] = dot(cv_t, prob.astype(jnp.bfloat16), NN)

    def pass_on(n):
        for quarter, base in ((4 + n, 0), (6 + n, 2)):
            kv_await(quarter, 1)
            for c in relay[n][base : base + 2]:
                c.start()

    def find_slots(j, carry):
        await_bytes(own_buf.at[j], o_rsem.at[j])
        copy = pltpu.make_async_copy(own_buf.at[j], raw, loc_sem.at[3])
        copy.start()
        copy.wait()
        for o in range(4):
            count, first, second = jnp.int32(0), jnp.int32(0), jnp.int32(0)
            for b in range(BRANCHES):
                hit = raw[b, 0] == group[o]
                for f in range(1, FAN):
                    hit = hit | (raw[b, f] == group[o])
                inv[(o * 4 + j) * BRANCHES + b] = jnp.where(hit & (count < 2), count, -1)
                first = jnp.where(hit & (count == 0), b, first)
                second = jnp.where(hit & (count == 1), b, second)
                count = count + hit.astype(jnp.int32)
            tab[slot_of(o, j, 0)] = first
            tab[slot_of(o, j, 1)] = second
        return carry

    def split_queries(j, carry):
        for b in range(BRANCHES):
            stacked = jnp.concatenate([qbuf[j, b, :, pl.ds(h * HEAD, HEAD)] for h in range(HEADS)], axis=0)
            exact = stacked.astype(jnp.float32) * SCALE
            high = exact.astype(jnp.bfloat16)
            qs[j * BRANCHES + b, :, :HEAD] = high
            qs[j * BRANCHES + b, :, HEAD:] = (exact - high.astype(jnp.float32)).astype(jnp.bfloat16)
        return carry

    def attend_round(i, carry):
        top, shrink = carry

        @pl.when(i == 0)
        def _():
            for n in (1, 2):
                await_bytes(qbuf.at[n], q_rsem.at[n])
                q_relay[n - 1].start()
            for c in closing:
                c.start()

        @pl.when(i == 1)
        def _():
            pass_on(0)
            await_bytes(qbuf.at[3, pl.ds(0, 2)], q_rsem.at[3])
            await_bytes(qbuf.at[3, pl.ds(2, 2)], q_rsem.at[4])
            pass_on(1)

        @pl.when(i < 2)
        def _():
            lax.fori_loop(1 + 2 * i, 3 + i, split_queries, 0)

        for n, quarter, count in ((3, 8, 2), (4, 10, 2), (5, 12, 1), (5, 14, 1)):

            @pl.when(i == n)
            def _():
                kv_await(quarter, count)

        for u in range(8):
            middle = step_of(i, u - 1) if u >= 1 else step_of(i - 1, 7)
            behind = step_of(i, u - 2) if u >= 2 else step_of(i - 1, 6 + u)
            top, shrink = advance(u, step_of(i, u), middle, behind, top, shrink)
        return top, shrink

    find_slots(0, 0)
    await_bytes(qbuf.at[0], q_rsem.at[0])
    split_queries(0, 0)
    opened = [step_of(-1, 4 + u) for u in range(4)]
    top = shrink = None
    for u in range(4):
        top, shrink = advance(
            u, opened[u], opened[u - 1] if u >= 1 else None, opened[u - 2] if u >= 2 else None, top, shrink
        )
    for c in opening[0] + opening[1]:
        c.start()
    own_rows()
    lax.fori_loop(1, 4, find_slots, 0)
    top, shrink = lax.fori_loop(0, 6, attend_round, (top, shrink))
    kv_await(13, 1)
    kv_await(15, 1)

    def ret_copies(j):
        return (
            remote(ret.at[j], back.at[mirror[j]], ret_ssem.at[0, j], ret_rsem.at[0, mirror[j]], peers[j]),
            remote(ret_lse.at[j], back_lse.at[mirror[j]], ret_ssem.at[1, j], ret_rsem.at[1, mirror[j]], peers[j]),
        )

    def finish(j):
        for b in range(BRANCHES):
            slots, tops, sums, oks = [], [], [], []
            for o in range(4):
                place = inv[(o * 4 + j) * BRANCHES + b]
                ok = place >= 0
                s = slot_of(o, j, jnp.where(ok, place, 0))
                slots.append(s)
                oks.append(ok)
                tops.append(jnp.where(ok, m_ref[s], LOW))
                sums.append(l_ref[s])
            peak = functools.reduce(jnp.maximum, tops)
            scales = [jnp.where(ok, jnp.exp2(t - peak), 0.0) for ok, t in zip(oks, tops)]
            denom = sum(a * l for a, l in zip(scales, sums))
            any_ok = denom > 0.0
            safe = jnp.where(any_ok, denom, 1.0)
            merged = sum(acc[s] * (a / safe) for s, a in zip(slots, scales))
            ret[j, b] = merged.astype(jnp.bfloat16)
            ret_lse[j, b : b + 1, :] = jnp.where(any_ok, peak + jnp.log(safe) * LOG2E, LOW)
        if j:
            for c in ret_copies(j):
                c.start()

    final = [step_of(5, 6), step_of(5, 7)]
    final += [(12, 2, 2 + u // 2, slot_of(3, 2 + u // 2, u % 2)) for u in range(4)]
    final += [last_step(u) for u in range(8)] + [None, None]
    for u in range(14):
        top, shrink = advance(u, final[u + 2], final[u + 1], final[u], top, shrink)
        if u >= 7 and u % 2:
            finish(3 - (u - 7) // 2)

    for n in (1, 2, 3):
        for c in ret_copies(n):
            c.wait_recv()

    for b in range(BRANCHES):
        lses = [own_m[b] + jnp.log(own_l[b]) * LOG2E, ret_lse[0, b : b + 1, :]]
        lses += [back_lse[n, b : b + 1, :] for n in (1, 2, 3)]
        peak = functools.reduce(jnp.maximum, lses)
        scales = [jnp.exp2(t - peak) for t in lses]
        denom = sum(scales)
        merged = own_acc[b] * (scales[0] / (denom * own_l[b]))
        outs = [ret[0, b]] + [back[n, b] for n in (1, 2, 3)]
        for a, o in zip(scales[1:], outs):
            merged = merged + o.astype(jnp.float32) * (a / denom)
        turned = jnp.transpose(merged).astype(jnp.bfloat16)
        for h in range(HEADS):
            attn[b * SLOTS : (b + 1) * SLOTS, h * HEAD : (h + 1) * HEAD] = turned[h * SLOTS : (h + 1) * SLOTS, :]
    copy_w.wait()

    width = w_buf.shape[1] // CHUNKS
    mid = width // 2
    share = part.shape[2]
    right, left, far = lax.rem(x + 1, 4), lax.rem(x + 3, 4), lax.rem(x + 2, 4)

    def pair_copy(n):
        return remote(pair_send.at[n], pair_recv.at[n], pair_ssem.at[n], pair_rsem.at[n], partner)

    def d_copies(n):
        return tuple(
            remote(d_send.at[n, i], d_recv.at[n, i], d_ssem.at[n, i], d_rsem.at[n, i], device)
            for i, device in ((0, x_right), (1, x_left))
        )

    def r_copy(n, i, half):
        return remote(
            r_send.at[n, i, half], r_recv.at[n, i, half], r_ssem.at[n, i, half], r_rsem.at[n, i, half],
            (x_right, x_left)[i],
        )

    def r_copies(n):
        return tuple(r_copy(n, i, half) for i in range(2) for half in range(2))

    def project(n):
        columns = pl.ds(pl.multiple_of(n * width, width), width)
        part[n] = dot(attn[...], w_buf[:, columns], NN).reshape(8, share, width)
        for i in range(4):
            pair_send[n, i] = part[n, 2 * i + 1 - core].astype(jnp.bfloat16)
        pair_copy(n).start()

    def pair_sum(n):
        pair_copy(n).wait_recv()
        for i in range(4):
            total[n, i] = part[n, 2 * i + core] + pair_recv[n, i].astype(jnp.float32)
        d_send[n, 0] = total[n, far, :, :mid].astype(jnp.bfloat16)
        d_send[n, 1] = total[n, far, :, mid:].astype(jnp.bfloat16)
        for c in d_copies(n):
            c.start()
        r_send[n, 0, 1] = total[n, right, :, mid:].astype(jnp.bfloat16)
        r_send[n, 1, 0] = total[n, left, :, :mid].astype(jnp.bfloat16)
        r_copy(n, 0, 1).start()
        r_copy(n, 1, 0).start()

    def ring_sum(n):
        for c in d_copies(n):
            c.wait_recv()
        r_send[n, 0, 0] = (total[n, right, :, :mid] + d_recv[n, 0].astype(jnp.float32)).astype(jnp.bfloat16)
        r_send[n, 1, 1] = (total[n, left, :, mid:] + d_recv[n, 1].astype(jnp.float32)).astype(jnp.bfloat16)
        r_copy(n, 0, 0).start()
        r_copy(n, 1, 1).start()

    def last_sum(n):
        for c in r_copies(n):
            c.wait_recv()
        for half in range(2):
            columns = pl.ds(pl.multiple_of(n * width + half * mid, mid), mid)
            out_ref[:, columns] = (
                total[n, x, :, half * mid : (half + 1) * mid]
                + r_recv[n, 0, half].astype(jnp.float32)
                + r_recv[n, 1, half].astype(jnp.float32)
            ).astype(jnp.bfloat16)

    def tail(i, carry):
        for lag, stage in zip(LAGS, (project, pair_sum, ring_sum, last_sum)):
            n = i - lag

            @pl.when((n >= 0) & (n < CHUNKS))
            def _():
                stage(n)

        return carry

    lax.fori_loop(0, CHUNKS + LAGS[-1], tail, 0)

    for c in sends:
        c.wait_send()
    for n in (1, 2, 3):
        for c in ret_copies(n):
            c.wait_send()

    def drain(n, carry):
        pair_copy(n).wait_send()
        for c in d_copies(n) + r_copies(n):
            c.wait_send()
        return carry

    lax.fori_loop(0, CHUNKS, drain, 0)


def body(queries, keys, values, own_keys, own_values, owners, lengths, out_weight):
    share = queries.shape[0] // 8
    depth, columns = out_weight.shape
    width = columns // CHUNKS
    mid = width // 2
    bf16, f32, i32 = jnp.bfloat16, jnp.float32, jnp.int32
    vmem = pltpu.VMEM
    dma = pltpu.SemaphoreType.DMA
    anywhere = pl.BlockSpec(memory_space=pl.ANY)
    inside = pl.BlockSpec(memory_space=pltpu.VMEM)
    scalars = pl.BlockSpec(memory_space=pltpu.SMEM)
    return pl.pallas_call(
        kernel,
        out_shape=jax.ShapeDtypeStruct((share, columns), bf16),
        in_specs=[anywhere, anywhere, anywhere, inside, inside, scalars, scalars, anywhere],
        out_specs=inside,
        scratch_shapes=[
            vmem((depth, columns), bf16),
            vmem((16, STRIP, HEAD), bf16),
            vmem((16, HEAD, STRIP), bf16),
            vmem((2 * HALF, HEAD), bf16),
            vmem((4, BRANCHES, SLOTS, HEADS * HEAD), bf16),
            vmem((4 * BRANCHES, COLS, 2 * HEAD), bf16),
            vmem((8, 128), i32),
            vmem((4, 8, 128), i32),
            pltpu.SMEM((8, 128), i32),
            pltpu.SMEM((32,), i32),
            pltpu.SMEM((64,), i32),
            vmem((HALF, COLS), f32),
            vmem((HALF, COLS), f32),
            vmem((HALF, COLS), bf16),
            vmem((HALF, COLS), bf16),
            vmem((32, 1, COLS), f32),
            vmem((32, 1, COLS), f32),
            vmem((32, HEAD, COLS), f32),
            vmem((BRANCHES, 1, COLS), f32),
            vmem((BRANCHES, 1, COLS), f32),
            vmem((BRANCHES, HEAD, COLS), f32),
            vmem((4, BRANCHES, HEAD, COLS), bf16),
            vmem((4, 8, COLS), f32),
            vmem((4, BRANCHES, HEAD, COLS), bf16),
            vmem((4, 8, COLS), f32),
            vmem((BRANCHES * SLOTS, depth), bf16),
            vmem((CHUNKS, 8, share, width), f32),
            vmem((CHUNKS, 4, share, width), f32),
            vmem((CHUNKS, 4, share, width), bf16),
            vmem((CHUNKS, 4, share, width), bf16),
            vmem((CHUNKS, 2, share, mid), bf16),
            vmem((CHUNKS, 2, share, mid), bf16),
            vmem((CHUNKS, 2, 2, share, mid), bf16),
            vmem((CHUNKS, 2, 2, share, mid), bf16),
            dma((4,)),
            dma((5,)), dma((5,)), dma((4,)), dma((4,)),
            dma((2, 16)), dma((2, 16)),
            dma((2, 4)), dma((2, 4)),
            dma((CHUNKS,)), dma((CHUNKS,)),
            dma((CHUNKS, 2)), dma((CHUNKS, 2)), dma((CHUNKS, 2, 2)), dma((CHUNKS, 2, 2)),
        ],
        compiler_params=pltpu.CompilerParams(
            collective_id=0, has_side_effects=True, vmem_limit_bytes=58 * 1024 * 1024
        ),
        name="branch_attention",
    )(
        queries.reshape(BRANCHES, SLOTS, queries.shape[1]),
        keys.reshape(4, STRIP, HEAD), values, own_keys, own_values, owners, lengths, out_weight,
    )


def solution(mesh):
    in_specs = (
        P("seq", "tp"),
        P("seq", "tp"),
        P("seq", "tp"),
        P("seq", "tp"),
        P("seq", "tp"),
        P("seq", None),
        P("seq"),
        P("tp", None),
    )
    out_specs = P(("seq", "tp"), None)
    return jax.shard_map(body, mesh=mesh, in_specs=in_specs, out_specs=out_specs, check_vma=False)
```

time: 74.7 us -> 64.4 us (0.86)
  Pallas kernels: 72.8 us -> 62.5 us
    pallas_call x1, Pallas kernels: 72.8 us -> 62.5 us  [body(): pl.pallas_call(kernel, out_shape=jax.ShapeDtypeStruct((share, columns), b...]
where the time goes in v2:
time: 64.4 us; the launch traced here: 64.2 us
  Pallas kernels  62.5 us (97%)
  local copies, waits for them, and re-layouts  1.67 us (3%)
    pallas_call x1, Pallas kernels, body(): pl.pallas_call(kernel, out_shape=jax.ShapeDtypeStruct((share, columns), b...  62.5 us
    unnamed x1, local copies, waits for them, and re-layouts  1.67 us

profile of v2, /device:TPU:1, one launch (start us, length us, event | category | flops | bytes accessed | tf_op | source)
XLA Modules:
  0.0 64.2 jit_solution(5340374126628807677)
XLA Ops:
  0.0 62.5 %branch_attention.1 = bf16[16,8192]{1,0:T(8,128)(2,1)} custom-call(bf16[4,32,1024]{2,1,0:T(8,128)(2,1)} %bitcast.3, bf16[4,512,128]{2,1,0:T(8,128)(2,1)} %bitcast.2, bf16[2048,128]{1,0:T(8,128)(2,1)} %v_hbm.1, bf16[128,128]{1,0:T(8,128)(2,1)} %ck_ref.1, bf16[128,128]{1,0:T(8,128)(2,1)} %cv_ref.1, s32[4,4]{1,0:T(4,128)} %owners_ref.1, s32[4]{0:T(128)} %lengths_ref.1, ...), custom_call_target="tpu_custom_call" | custom-call | tf_op jit(solution)/shard_map/branch_attention/pallas_call | solution.py:464
  62.6 1.7 %copy.10 = bf16[16,8192]{1,0:T(8,128)(2,1)} copy(bf16[16,8192]{1,0:T(8,128)(2,1)} %branch_attention.1) | data formatting | bytes 524288

commit v3 on v2

--- a/solution.py
+++ b/solution.py
@@ -182,17 +182,14 @@
             best = jnp.max(best.reshape(8, 8, COLS), axis=0)
         return best, next_shrink
 
-    def step_of(i, u):
-        own = 1 - lax.div(i + (6 if u < 4 else 7), 8)
-        piece = (1 - own) * (i - (2 if u < 4 else 1))
-        far = lax.div(piece, 4)
-        quarter = own * 2 * (u % 4 // 2) + (1 - own) * (4 + 2 * piece)
-        owner = (1 - own) * ((1 - far) * (1 + lax.rem(piece, 2)) + 3 * far)
-        j = own * (2 * i + (1 if u < 4 else 2)) + (1 - own) * ((2 if u < 4 else 0) + u % 4 // 2)
-        return quarter, 1 + far, j, slot_of(owner, j, u % 2)
-
-    def last_step(u):
-        return 13, 2, 3 - u // 2, slot_of(3, 3 - u // 2, u % 2)
+    def own_step(j, u):
+        return 2 * (u // 2), 1, j, slot_of(0, j, u % 2)
+
+    def near_step(piece, u):
+        return 4 + 2 * piece, 1, u // 2, slot_of(1 + lax.rem(piece, 2), u // 2, u % 2)
+
+    def far_step(j, u):
+        return 12 + u // 2, 2, j, slot_of(3, j, u % 2)
 
     scores_of, probs_of = (s_a, s_b), (p_a, p_b)
 
@@ -254,10 +251,10 @@
             qs[j * BRANCHES + b, :, HEAD:] = (exact - high.astype(jnp.float32)).astype(jnp.bfloat16)
         return carry
 
-    def attend_round(i, carry):
+    def own_round(j, carry):
         top, shrink = carry
 
-        @pl.when(i == 0)
+        @pl.when(j == 1)
         def _():
             for n in (1, 2):
                 await_bytes(qbuf.at[n], q_rsem.at[n])
@@ -265,33 +262,42 @@
             for c in closing:
                 c.start()
 
-        @pl.when(i == 1)
+        @pl.when(j == 3)
         def _():
             pass_on(0)
             await_bytes(qbuf.at[3, pl.ds(0, 2)], q_rsem.at[3])
             await_bytes(qbuf.at[3, pl.ds(2, 2)], q_rsem.at[4])
-            pass_on(1)
-
-        @pl.when(i < 2)
-        def _():
-            lax.fori_loop(1 + 2 * i, 3 + i, split_queries, 0)
-
-        for n, quarter, count in ((3, 8, 2), (4, 10, 2), (5, 12, 1), (5, 14, 1)):
-
-            @pl.when(i == n)
+
+        split_queries(j, 0)
+        steps = [own_step(j - 1, 2), own_step(j - 1, 3)] + [own_step(j, u) for u in range(4)]
+        for u in range(4):
+            top, shrink = advance(u, steps[u + 2], steps[u + 1], steps[u], top, shrink)
+        return top, shrink
+
+    def near_round(piece, carry):
+        top, shrink = carry
+        start = 1 - lax.div(piece + 3, 4)
+        before = piece - 1 + start
+
+        for n, quarter in ((2, 8), (3, 10)):
+
+            @pl.when(piece == n)
             def _():
-                kv_await(quarter, count)
-
+                kv_await(quarter, 2)
+
+        def earlier(u):
+            near, own = near_step(before, u), own_step(3, u - 4)
+            return tuple(start * b + (1 - start) * a for a, b in zip(near, own))
+
+        steps = [earlier(6), earlier(7)] + [near_step(piece, u) for u in range(8)]
         for u in range(8):
-            middle = step_of(i, u - 1) if u >= 1 else step_of(i - 1, 7)
-            behind = step_of(i, u - 2) if u >= 2 else step_of(i - 1, 6 + u)
-            top, shrink = advance(u, step_of(i, u), middle, behind, top, shrink)
+            top, shrink = advance(u, steps[u + 2], steps[u + 1], steps[u], top, shrink)
         return top, shrink
 
     find_slots(0, 0)
     await_bytes(qbuf.at[0], q_rsem.at[0])
     split_queries(0, 0)
-    opened = [step_of(-1, 4 + u) for u in range(4)]
+    opened = [own_step(0, u) for u in range(4)]
     top = shrink = None
     for u in range(4):
         top, shrink = advance(
@@ -301,9 +307,9 @@
         c.start()
     own_rows()
     lax.fori_loop(1, 4, find_slots, 0)
-    top, shrink = lax.fori_loop(0, 6, attend_round, (top, shrink))
-    kv_await(13, 1)
-    kv_await(15, 1)
+    carry = lax.fori_loop(1, 4, own_round, (top, shrink))
+    pass_on(1)
+    top, shrink = lax.fori_loop(0, 4, near_round, carry)
 
     def ret_copies(j):
         return (
@@ -334,13 +340,15 @@
             for c in ret_copies(j):
                 c.start()
 
-    final = [step_of(5, 6), step_of(5, 7)]
-    final += [(12, 2, 2 + u // 2, slot_of(3, 2 + u // 2, u % 2)) for u in range(4)]
-    final += [last_step(u) for u in range(8)] + [None, None]
-    for u in range(14):
+    final = [near_step(3, 6), near_step(3, 7)]
+    final += [far_step(j, u) for j in (3, 2, 1, 0) for u in range(4)] + [None, None]
+    for u in range(18):
+        if u in (0, 2):
+            kv_await(12 + u // 2, 1)
+            kv_await(14 + u // 2, 1)
         top, shrink = advance(u, final[u + 2], final[u + 1], final[u], top, shrink)
-        if u >= 7 and u % 2:
-            finish(3 - (u - 7) // 2)
+        if u >= 5 and u % 4 == 1:
+            finish(3 - (u - 5) // 4)
 
     for n in (1, 2, 3):
         for c in ret_copies(n):

time: 64.4 us -> 62.2 us (0.966)
  Pallas kernels: 62.5 us -> 60.3 us
    pallas_call x1, Pallas kernels: 62.5 us -> 60.3 us  [body(): pl.pallas_call(kernel, out_shape=jax.ShapeDtypeStruct((share, columns), b...]
where the time goes in v3:
time: 62.2 us; the launch traced here: 62 us
  Pallas kernels  60.3 us (97%)
  local copies, waits for them, and re-layouts  1.67 us (3%)
    pallas_call x1, Pallas kernels, body(): pl.pallas_call(kernel, out_shape=jax.ShapeDtypeStruct((share, columns), b...  60.3 us
    unnamed x1, local copies, waits for them, and re-layouts  1.67 us

profile of v3, /device:TPU:1, one launch (start us, length us, event | category | flops | bytes accessed | tf_op | source)
XLA Modules:
  0.0 62.0 jit_solution(6502363578852189653)
XLA Ops:
  0.0 60.3 %branch_attention.1 = bf16[16,8192]{1,0:T(8,128)(2,1)} custom-call(bf16[4,32,1024]{2,1,0:T(8,128)(2,1)} %bitcast.3, bf16[4,512,128]{2,1,0:T(8,128)(2,1)} %bitcast.2, bf16[2048,128]{1,0:T(8,128)(2,1)} %v_hbm.1, bf16[128,128]{1,0:T(8,128)(2,1)} %ck_ref.1, bf16[128,128]{1,0:T(8,128)(2,1)} %cv_ref.1, s32[4,4]{1,0:T(4,128)} %owners_ref.1, s32[4]{0:T(128)} %lengths_ref.1, ...), custom_call_target="tpu_custom_call" | custom-call | tf_op jit(solution)/shard_map/branch_attention/pallas_call | solution.py:472
  60.3 1.7 %copy.10 = bf16[16,8192]{1,0:T(8,128)(2,1)} copy(bf16[16,8192]{1,0:T(8,128)(2,1)} %branch_attention.1) | data formatting | bytes 524288

commit v4 on v3

--- a/solution.py
+++ b/solution.py
@@ -95,6 +95,9 @@
     copy_v.wait()
     for n in (0, 2, 1, 3):
         vp[n] = jnp.transpose(v_own[pl.ds(n * STRIP, STRIP), :].astype(jnp.float32)).astype(jnp.bfloat16)
+    m_ref[...] = jnp.full(m_ref.shape, LOW, jnp.float32)
+    l_ref[...] = jnp.zeros(l_ref.shape, jnp.float32)
+    acc[...] = jnp.zeros(acc.shape, jnp.float32)
     pl.semaphore_wait(barrier, len(everyone))
 
     sends = []
@@ -140,10 +143,6 @@
     copy_k.wait()
     copy_w = pltpu.make_async_copy(w_hbm, w_buf, loc_sem.at[2])
     copy_w.start()
-
-    m_ref[...] = jnp.full(m_ref.shape, LOW, jnp.float32)
-    l_ref[...] = jnp.zeros(l_ref.shape, jnp.float32)
-    acc[...] = jnp.zeros(acc.shape, jnp.float32)
 
     def slot_of(o, j, k):
         return o * 8 + j * 2 + k

time: 62.2 us -> 62.5 us (level)
  no operation moved by 1% of the time
where the time goes in v4:
time: 62.5 us; the launch traced here: 62.3 us
  Pallas kernels  60.6 us (97%)
  local copies, waits for them, and re-layouts  1.67 us (3%)
    pallas_call x1, Pallas kernels, body(): pl.pallas_call(kernel, out_shape=jax.ShapeDtypeStruct((share, columns), b...  60.6 us
    unnamed x1, local copies, waits for them, and re-layouts  1.67 us

profile of v4, /device:TPU:1, one launch (start us, length us, event | category | flops | bytes accessed | tf_op | source)
XLA Modules:
  0.0 62.3 jit_solution(7057633701335560669)
XLA Ops:
  0.0 60.6 %branch_attention.1 = bf16[16,8192]{1,0:T(8,128)(2,1)} custom-call(bf16[4,32,1024]{2,1,0:T(8,128)(2,1)} %bitcast.3, bf16[4,512,128]{2,1,0:T(8,128)(2,1)} %bitcast.2, bf16[2048,128]{1,0:T(8,128)(2,1)} %v_hbm.1, bf16[128,128]{1,0:T(8,128)(2,1)} %ck_ref.1, bf16[128,128]{1,0:T(8,128)(2,1)} %cv_ref.1, s32[4,4]{1,0:T(4,128)} %owners_ref.1, s32[4]{0:T(128)} %lengths_ref.1, ...), custom_call_target="tpu_custom_call" | custom-call | tf_op jit(solution)/shard_map/branch_attention/pallas_call | solution.py:471
  60.6 1.7 %copy.10 = bf16[16,8192]{1,0:T(8,128)(2,1)} copy(bf16[16,8192]{1,0:T(8,128)(2,1)} %branch_attention.1) | data formatting | bytes 524288
